TPU v7x, 512 devices: a whole 4x4x16 slice. The times are simulated.
512 devices in a mesh: dp: 32 (over z, core), fsdp: 16 (over x, y).
Axes of the slice: x: 4, y: 4, z: 16, core: 2. Of those that a mesh axis runs over, the one named last changes fastest.
Arguments:
- counts: int32 [512], P(('dp', 'fsdp')), may hold values from 1 to 4
- tokens: bfloat16 [65536, 8192], P(('dp', 'fsdp')), may hold values from -24 to 24
- queries: bfloat16 [65536, 4096], P(('dp', 'fsdp')), may hold values from -6 to 6
- values: bfloat16 [65536, 512], P(('dp', 'fsdp')), may hold values from -6 to 6
- out_grad: bfloat16 [65536, 4096], P(('dp', 'fsdp')), may hold values from -6 to 6
- key_codes: bfloat16 [8192, 512], P('fsdp'), may hold values from -4 to 4
- key_scales: float32 [8192, 2], P('fsdp'), may hold values from 0.0044194176 to 0.027621359
Outputs:
- key_grad: float32 [8192, 512], P(('fsdp', 'dp'))
Inputs may be any that keep to these rules, and one draw needn't show every extreme that they name: counts[r] is how many of device r's 4 microbatch slots hold a live microbatch (the first ones).
All inputs are finite; a program needn't handle non-finite values.
Results may differ from a plain program's by a relative error of at most 0.039.
Values may be sent and summed in bfloat16 or wider, within the bound.
A program may use at most 128 MiB of HBM per device.

v0:
```python
import math

import jax
import jax.numpy as jnp
from jax import lax
from jax.sharding import PartitionSpec as P

HD = 128
MB_MAX = 4


def dequantize(code_rows, scales):
    row_count = code_rows.shape[0]
    blocks = scales.shape[1]
    widened = code_rows.astype(jnp.float32).reshape(row_count, blocks, -1) * scales[:, :, None]
    return widened.reshape(row_count, -1).astype(jnp.bfloat16)


def key_delta_rows(queries, key_rows, values, out_grad, live_count):
    slot_count = MB_MAX
    length = queries.shape[0] // slot_count
    kv_heads = key_rows.shape[1] // HD
    group_size = queries.shape[1] // key_rows.shape[1]
    inverse = 1.0 / math.sqrt(HD)
    query_b = queries.reshape(slot_count, length, kv_heads, group_size, HD)
    key_b = key_rows.reshape(slot_count, length, kv_heads, HD)
    value_b = values.reshape(slot_count, length, kv_heads, HD)
    grad_b = out_grad.reshape(slot_count, length, kv_heads, group_size, HD)
    scores = (
        jnp.einsum("mqhgd,mkhd->mhgqk", query_b, key_b, preferred_element_type=jnp.float32)
        * inverse
    )
    position = jnp.arange(length)
    causal = (position[:, None] >= position[None, :]).astype(jnp.float32)
    attention = jnp.exp(scores) * causal
    attention = attention / jnp.sum(attention, axis=-1, keepdims=True)
    prob_grad = jnp.einsum("mqhgd,mkhd->mhgqk", grad_b, value_b, preferred_element_type=jnp.float32)
    row_delta = jnp.sum(attention * prob_grad, axis=-1, keepdims=True)
    dscore = (attention * (prob_grad - row_delta)).astype(jnp.bfloat16)
    key_grad = (
        jnp.einsum("mhgqk,mqhgd->mkhd", dscore, query_b, preferred_element_type=jnp.float32)
        * inverse
    )
    live_slot = (jnp.arange(slot_count) < live_count).astype(jnp.float32)
    key_grad = key_grad * live_slot[:, None, None, None]
    return key_grad.reshape(slot_count * length, kv_heads * HD).astype(jnp.bfloat16)


def local(counts, tokens, queries, values, out_grad, key_codes, key_scales):
    tok_rows = tokens.shape[0]
    share_rows = key_codes.shape[0]
    key_width = key_codes.shape[1]
    groups = lax.axis_size("fsdp")
    replicas = lax.axis_size("dp")
    columns = lax.all_to_all(tokens, "fsdp", split_axis=1, concat_axis=0, tiled=True)
    weight = dequantize(
        lax.all_gather(key_codes, "fsdp", axis=0, tiled=True),
        lax.all_gather(key_scales.astype(jnp.bfloat16), "fsdp", axis=0, tiled=True).astype(
            jnp.float32
        ),
    )
    summed = jnp.dot(tokens, weight, preferred_element_type=jnp.float32)
    key_rows = summed.astype(jnp.bfloat16)
    key_delta = key_delta_rows(queries, key_rows, values, out_grad, counts[0])
    section_sum = lax.dot_general(
        columns,
        lax.all_gather(key_delta, "fsdp", axis=0, tiled=True),
        (((0,), (0,)), ((), ())),
        preferred_element_type=jnp.float32,
    )
    section_split = section_sum.reshape(replicas, share_rows // replicas, key_width)
    arrived = lax.all_to_all(
        section_split.astype(jnp.bfloat16), "dp", split_axis=0, concat_axis=0, tiled=True
    ).astype(section_split.dtype)
    running = jnp.sum(arrived, axis=0)
    factor = 1.0 / math.sqrt(replicas * groups * tok_rows)
    return running * factor


def solution(mesh):
    return jax.shard_map(
        local,
        mesh=mesh,
        in_specs=(
            P(("dp", "fsdp")),
            P(("dp", "fsdp"), None),
            P(("dp", "fsdp"), None),
            P(("dp", "fsdp"), None),
            P(("dp", "fsdp"), None),
            P("fsdp", None),
            P("fsdp", None),
        ),
        out_specs=P(("fsdp", "dp"), None),
        check_vma=False,
    )
```

profile of v0, /device:TPU:1, one launch (start us, length us, event | category | flops | bytes accessed | tf_op | source)
XLA Modules:
  0.0 243.0 jit_solution(2622163456651071260)
XLA Ops:
  6.5 0.0 copy-start.4
  6.5 0.0 all-gather.3.cloned.1.call-start
  6.5 0.7 all-gather.3.cloned.1.call-update
  7.3 0.0 all-gather.5.cloned.1.call-start
  7.3 1.4 copy.40
  8.8 0.0 copy-done.4
  8.8 19.2 %all_gather.10 = bf16[8192,2]{0,1:T(2,128)(2,1)S(1)} all-gather(bf16[512,2]{0,1:T(2,128)(2,1)S(1)} %convert_element_type.55), channel_id=1, replica_groups=mesh['dp'=32,'fsdp'=16] {'fsdp'}, dimensions={0}, use_global_device_ids=true | all-gather | bytes 34816 | tf_op jit(solution)/shard_map/all_gather | solution.py:58
  28.0 2.4 copy.22
  30.4 11.0 %mul.53 = f32[8192,2,256]{2,1,0:T(2,128)S(1)} broadcast(f32[8192,2]{1,0:T(8,128)} %copy.22), dimensions={0,1} | broadcast | bytes 16842752 | tf_op jit(solution)/shard_map/mul | solution.py:15
  41.3 0.0 copy-start.1
  41.4 0.0 copy-start.3
  41.4 7.2 %copy.39 = f32[1024,8,2,256]{3,1,2,0:T(8,128)} copy(f32[1024,8,2,256]{3,2,1,0:T(2,128)S(1)} %bitcast.60) | data formatting | bytes 33554432
  48.6 0.0 copy-start
  48.6 0.0 copy-done.1
  48.6 1.3 copy.41
  49.8 0.0 copy-done.3
  50.5 0.6 compare_select_fusion
  51.1 50.6 %all-gather.3.cloned.1.call-done = bf16[8192,512]{1,0:T(8,128)(2,1)} async-done(((bf16[512,512]{1,0:T(8,128)(2,1)}), bf16[8192,512]{1,0:T(8,128)(2,1)}) %all-gather.3.cloned.1.call-update) | async-done | bytes 8388624 | tf_op jit(solution)/shard_map/all_gather | solution.py:57
  101.8 0.0 copy-done
  101.8 11.4 %fusion.10 = bf16[128,512]{0,1:T(8,128)(2,1)S(1)} fusion(bf16[128,8192]{1,0:T(8,128)(2,1)S(1)} %copy-done, f32[8192,512]{1,0:T(8,128)} %bitcast.61, bf16[8192,512]{1,0:T(8,128)(2,1)} %all-gather.3.cloned.1.call-done), kind=kOutput, calls=%fused_computation.16 | convolution fusion | flops 1086390272 | bytes 27394048 | tf_op jit(solution)/shard_map/dot_general | solution.py:62
  113.2 0.1 copy.23
  113.4 0.0 copy-start.2
  113.4 1.8 fusion.5
  115.2 0.0 copy-done.2
  115.2 0.0 copy-start.5
  115.2 1.8 fusion.1
  117.1 0.0 copy-done.5
  117.1 1.1 fusion.9
  118.2 0.1 copy.29
  118.3 0.7 copy.62
  119.0 0.0 all-gather.5.cloned.1.call-update
  119.0 2.5 %copy.30 = bf16[128,8192]{0,1:T(8,128)(2,1)} copy(bf16[128,8192]{1,0:T(8,128)(2,1)S(1)} %copy-done) | data formatting | bytes 4194304 | tf_op args[1]
  121.4 34.2 %all_to_all.24 = bf16[128,16,512]{0,2,1:T(8,128)(2,1)S(1)} all-to-all(bf16[128,16,512]{0,2,1:T(8,128)(2,1)} %bitcast.63), channel_id=1, replica_groups=mesh['dp'=32,'fsdp'=16] {'fsdp'}, dimensions={1} | all-to-all | bytes 4194304 | tf_op jit(solution)/shard_map/all_to_all | solution.py:55
  155.6 2.6 %copy.31 = bf16[16,128,512]{2,1,0:T(8,128)(2,1)} copy(bf16[16,128,512]{1,2,0:T(8,128)(2,1)S(1)} %bitcast.62) | data formatting | bytes 4194304 | tf_op jit(solution)/shard_map/all_to_all | solution.py:55
  158.2 26.5 %all-gather.5.cloned.1.call-done = bf16[2048,512]{1,0:T(8,128)(2,1)} async-done(((bf16[128,512]{1,0:T(8,128)(2,1)}), bf16[2048,512]{1,0:T(8,128)(2,1)}) %all-gather.5.cloned.1.call-update) | async-done | bytes 2097168 | tf_op jit(solution)/shard_map/all_gather | solution.py:67
  184.7 3.5 %convolution_convert_fusion = bf16[512,512]{0,1:T(8,128)(2,1)S(1)} fusion(bf16[2048,512]{1,0:T(8,128)(2,1)} %all-gather.5.cloned.1.call-done, bf16[2048,512]{1,0:T(8,128)(2,1)} %bitcast.66), kind=kOutput, calls=%fused_computation.10 | convolution fusion | flops 1074003968 | bytes 4718592 | tf_op jit(solution)/shard_map/dot_general | solution.py:65
  188.3 47.2 %all_to_all.25 = bf16[32,16,512]{2,1,0:T(8,128)(2,1)S(1)} all-to-all(bf16[32,16,512]{2,1,0:T(8,128)(2,1)S(1)} %bitcast.71), channel_id=1, replica_groups=mesh['dp'=32,'fsdp'=16] {'dp'}, dimensions={0} | all-to-all | bytes 1048576 | tf_op jit(solution)/shard_map/all_to_all | solution.py:72
  235.4 0.1 convert_reduce_fusion
  235.5 0.6 broadcast_multiply_fusion
  (4 shorter events, 0.1 us)
Async XLA Ops:
  6.5 2.2 copy-start.4
  6.5 95.2 %all-gather.3.cloned.1.call-start = ((), (), s32[]{:S(2)}) async-start(), calls=%async_computation.2 | async-start | bytes 8912896 | tf_op jit(solution)/shard_map/all_gather | solution.py:57
  7.3 177.5 %all-gather.5.cloned.1.call-start = ((), (), s32[]{:S(2)}) async-start(), calls=%async_computation.3 | async-start | bytes 2228224 | tf_op jit(solution)/shard_map/all_gather | solution.py:67
  41.3 7.2 %copy-start.1 = (bf16[128,4096]{1,0:T(8,128)(2,1)S(1)}, bf16[128,4096]{1,0:T(8,128)(2,1)}, u32[]{:S(2)}) copy-start(bf16[128,4096]{1,0:T(8,128)(2,1)} %param.11) | copy-start | bytes 3145732
  41.4 8.5 %copy-start.3 = (bf16[128,512]{1,0:T(8,128)(2,1)S(1)}, bf16[128,512]{1,0:T(8,128)(2,1)}, u32[]{:S(2)}) copy-start(bf16[128,512]{1,0:T(8,128)(2,1)} %param.10) | copy-start | bytes 393220
  48.6 53.2 %copy-start = (bf16[128,8192]{1,0:T(8,128)(2,1)S(1)}, bf16[128,8192]{1,0:T(8,128)(2,1)}, u32[]{:S(2)}) copy-start(bf16[128,8192]{1,0:T(8,128)(2,1)} %param.8) | copy-start | bytes 6291460
  113.4 1.8 copy-start.2
  115.2 1.9 copy-start.5
Sparse Core Ops, SparseCore 0:
  10.4 91.3 all-gather.2
  119.1 65.5 all-gather.4
where the time goes:
time: 243 us
  blocking collectives  101 us (42%)
  waiting for transfers between devices  77.9 us (32%)
  local copies, waits for them, and re-layouts  29.2 us (12%)
  matrix products  19.7 us (8%)
  between operations  14.2 us (6%)
    all_gather x1, waiting for transfers between devices, local(): lax.all_gather(key_codes, 'fsdp', axis=0, tiled=True)  50.6 us
    all_to_all x1, blocking collectives, local(): lax.all_to_all(section_split.astype(jnp.bfloat16), 'dp', split_axis=0, co...  47.2 us
    all_to_all x1, blocking collectives, local(): lax.all_to_all(tokens, 'fsdp', split_axis=1, concat_axis=0, tiled=True)  34.2 us
    all_gather x1, waiting for transfers between devices, local(): lax.all_gather(key_delta, 'fsdp', axis=0, tiled=True)  26.5 us
    all_gather x1, blocking collectives, local(): lax.all_gather(key_scales.astype(jnp.bfloat16), 'fsdp', axis=0, tiled=True)  19.2 us
    unnamed x17, local copies, waits for them, and re-layouts  13.1 us
    dot_general x1, matrix products, local(): summed = jnp.dot(tokens, weight, preferred_element_type=jnp.float32)  11.4 us
    mul x1, local copies, waits for them, and re-layouts, dequantize(): code_rows.astype(jnp.float32).reshape(row_count, blocks, -1)  11 us
  transfers between devices with their start and end apart: 2, of which 2 were waited for; matrix products, arithmetic and copies ran while one was open for 12% of the time, Pallas kernels for 0%

commit v1 on v0

v1 whole, which is shorter than its diff:
```python
import functools
import math

import jax
import jax.numpy as jnp
from jax import lax
from jax.experimental import pallas as pl
from jax.experimental.pallas import tpu as pltpu
from jax.sharding import PartitionSpec as P

MESH = pl.DeviceIdType.MESH
F32 = jnp.float32
BF16 = jnp.bfloat16
HD = 128
RING = 4
TOK = 128
MB = 32
SHARD = 512
HALF = 256
QUARTER = 128
GROUP = 8
QW = 2048
OFFSETS = (2, 1, -1, 0)


def kernel(
    nz,
    counts,
    tokens,
    queries,
    values,
    out_grad,
    codes,
    scales,
    out,
    codes_v,
    scales_v,
    cnt,
    tok,
    tok_t,
    q2,
    v2,
    og2,
    wbuf,
    acc,
    keys,
    delta,
    part,
    rs_send,
    rs_recv,
    z_send,
    z_recv,
    swap_send,
    swap_recv,
    load_sem,
    core_send,
    core_recv,
    ag_send,
    ag_recv,
    r_send,
    r_recv,
    zs_sem,
    zr_sem,
):
    dp = lax.axis_index("dp")
    f = lax.axis_index("fsdp")
    x, y = f // RING, f % RING
    z, core = dp // 2, dp % 2
    other = 1 - core
    partner = (2 * z + other, f)

    def wrap(v):
        return (v + 2 * RING) % RING

    def chip(dx, dy):
        return (dp, wrap(x + dx) * RING + wrap(y + dy))

    def along(half, axis, step):
        if half == axis:
            return chip(step, 0)
        return chip(0, step)

    def block(half, d1, d2):
        dx = d1 * (1 - half) + d2 * half
        dy = d2 * (1 - half) + d1 * half
        return wrap(x + dx) * RING + wrap(y + dy)

    def z_peer(i):
        return (((z + i) % nz) * 2 + core, f)

    mine = pl.ds(pl.multiple_of(core * HALF, HALF), HALF)
    theirs = pl.ds(pl.multiple_of(other * HALF, HALF), HALF)
    mine_q = pl.ds(pl.multiple_of(core * QW, QW), QW)
    theirs_q = pl.ds(pl.multiple_of(other * QW, QW), QW)
    low, high = pl.ds(0, TOK), pl.ds(TOK, TOK)
    loads = [
        pltpu.make_async_copy(src, dst, load_sem.at[i])
        for i, (src, dst) in enumerate(
            [
                (codes.at[:, mine], codes_v),
                (scales, scales_v),
                (tokens, tok.at[low]),
                (queries.at[:, mine_q], q2.at[low]),
                (values.at[:, mine], v2.at[low]),
                (out_grad.at[:, mine_q], og2.at[low]),
            ]
        )
    ]
    for load in loads:
        load.start()
    cnt[0] = jnp.full((8, 128), counts[0], jnp.int32)

    barrier = pltpu.get_barrier_semaphore()
    neighbours = [partner, chip(1, 0), chip(-1, 0), chip(0, 1), chip(0, -1)]
    for device in neighbours:
        pl.semaphore_signal(barrier, inc=1, device_id=device, device_id_type=MESH)

    def greet(i, carry):
        pl.semaphore_signal(barrier, inc=1, device_id=z_peer(i), device_id_type=MESH)
        return carry

    lax.fori_loop(1, nz, greet, 0)

    loads[0].wait()
    loads[1].wait()
    scale = jnp.where(core == 0, scales_v[:, 0:1], scales_v[:, 1:2])
    weight = (codes_v[...].astype(F32) * scale).astype(BF16)
    wbuf[f, 0] = weight[:HALF]
    wbuf[f, 1] = weight[HALF:]

    pl.semaphore_wait(barrier, len(neighbours) + nz - 1)

    def remote(src, dst, send, recv, device):
        return pltpu.make_async_remote_copy(
            src_ref=src,
            dst_ref=dst,
            send_sem=send,
            recv_sem=recv,
            device_id=device,
            device_id_type=MESH,
        )

    upper, lower = pl.ds(0, QUARTER), pl.ds(QUARTER, QUARTER)
    whole = pl.ds(0, HALF)
    ag_sent = []

    def ag_copy(half, index, o, rows, axis, step):
        k = half * 20 + index
        ref = wbuf.at[o, half, rows]
        return remote(ref, ref, ag_send.at[k], ag_recv.at[k], along(half, axis, step))

    def ag_start(*args):
        copy = ag_copy(*args)
        copy.start()
        ag_sent.append(copy)

    def ag_wait(half, index, rows):
        ag_copy(half, index, f, rows, 0, 1).wait_recv()

    FIRST = (0, -1, 1, 2)

    def both(half, index, d1, d2, axis):
        ag_start(half, index, block(half, d1, d2), whole, axis, 1)
        ag_start(half, index + 1, block(half, d1, d2), whole, axis, -1)

    for half in (0, 1):
        both(half, 0, 0, 0, 0)
    for half in (0, 1):
        both(half, 4, 0, 0, 1)

    core_copies = [
        remote(src, dst, core_send.at[i], core_recv.at[i], partner)
        for i, (src, dst) in enumerate(
            [
                (tokens, tok.at[high]),
                (queries.at[:, theirs_q], q2.at[high]),
                (out_grad.at[:, theirs_q], og2.at[high]),
                (values.at[:, theirs], v2.at[high]),
                (cnt.at[0], cnt.at[1]),
            ]
        )
    ]
    for copy in core_copies:
        copy.start()

    def project(d1, d2):
        def body(half, carry):
            o = block(half, d1, d2)
            columns = pl.ds(pl.multiple_of(o * SHARD + half * HALF, HALF), HALF)
            acc[...] += jnp.dot(tok[:, columns], wbuf[o, half], preferred_element_type=F32)
            return carry

        lax.fori_loop(0, 2, body, 0)

    def transpose(first, last):
        def body(k, carry):
            piece = pl.ds(pl.multiple_of(k * HALF, HALF), HALF)
            tok_t[piece, :] = tok[:, piece].T
            return carry

        lax.fori_loop(first, last, body, 0)

    def first_pass():
        for half in (0, 1):
            ag_wait(half, 0, whole)
            ag_start(half, 2, block(half, -1, 0), upper, 0, 1)
            both(half, 8, -1, 0, 1)
            ag_wait(half, 1, whole)
            ag_start(half, 3, block(half, 1, 0), lower, 0, -1)
            both(half, 12, 1, 0, 1)

    def second_pass(j):
        for half in (0, 1):
            base = 4 + 4 * j
            ag_wait(half, base, whole)
            ag_start(half, base + 2, block(half, FIRST[j], -1), upper, 1, 1)
            ag_wait(half, base + 1, whole)
            ag_start(half, base + 3, block(half, FIRST[j], 1), lower, 1, -1)

    def second_end(j):
        for half in (0, 1):
            ag_wait(half, 4 + 4 * j + 2, upper)
            ag_wait(half, 4 + 4 * j + 3, lower)

    acc[...] = jnp.zeros_like(acc)
    first_pass()
    loads[2].wait()
    core_copies[0].wait_recv()
    project(0, 0)
    project(-1, 0)
    project(1, 0)
    transpose(0, 8)
    second_pass(0)
    project(0, -1)
    project(0, 1)
    for half in (0, 1):
        ag_wait(half, 2, upper)
        ag_wait(half, 3, lower)
        both(half, 16, 2, 0, 1)
    project(2, 0)
    transpose(8, 16)
    second_pass(1)
    project(-1, -1)
    project(-1, 1)
    second_end(0)
    project(0, 2)
    transpose(16, 24)
    second_pass(2)
    project(1, -1)
    project(1, 1)
    second_end(1)
    project(-1, 2)
    transpose(24, 32)
    second_pass(3)
    second_end(2)
    project(1, 2)
    project(2, -1)
    project(2, 1)
    second_end(3)
    project(2, 2)
    keys[...] = acc[...].astype(BF16)

    for load in loads[3:]:
        load.wait()
    for copy in core_copies[1:]:
        copy.wait_recv()
    inverse = 1.0 / math.sqrt(HD)
    key_at = lax.broadcasted_iota(jnp.int32, (MB, GROUP * MB), 0)
    query_at = lax.broadcasted_iota(jnp.int32, (MB, GROUP * MB), 1) % MB
    seen = key_at <= query_at
    contract_last = (((1,), (1,)), ((), ()))

    def microbatch(m, carry):
        rows = pl.ds(pl.multiple_of(m * MB, MB), MB)
        live = (m % 4) < cnt[m // 4][0:1]
        for head in range(2):
            columns = pl.ds(head * HD, HD)
            start = head * GROUP * HD
            query = jnp.concatenate(
                [q2[rows, pl.ds(start + g * HD, HD)] for g in range(GROUP)], axis=0
            )
            grad = jnp.concatenate(
                [og2[rows, pl.ds(start + g * HD, HD)] for g in range(GROUP)], axis=0
            )
            scores = lax.dot_general(
                keys[rows, columns], query, contract_last, preferred_element_type=F32
            )
            weights = jnp.where(seen, jnp.exp(scores * inverse), 0.0)
            probs = weights / jnp.sum(weights, axis=0, keepdims=True)
            prob_grad = lax.dot_general(
                v2[rows, columns], grad, contract_last, preferred_element_type=F32
            )
            row_delta = jnp.sum(probs * prob_grad, axis=0, keepdims=True)
            dscore = (probs * (prob_grad - row_delta)).astype(BF16)
            key_grad = jnp.dot(dscore, query, preferred_element_type=F32) * inverse
            delta[rows, columns] = jnp.where(live, key_grad, 0.0).astype(BF16)
        return carry

    lax.fori_loop(0, 2 * TOK // MB, microbatch, 0)

    rs_sent = []

    def rs_copy(half, n, index):
        k = (half * 5 + n) * 6 + index
        axis = 0 if n < 4 else 1
        return remote(
            rs_send.at[half, n, index],
            rs_recv.at[half, n, index],
            r_send.at[k],
            r_recv.at[k],
            along(half, axis, 1 if index % 2 == 0 else -1),
        )

    def rs_start(half, n, index, value):
        rs_send[half, n, index] = value.astype(BF16)
        copy = rs_copy(half, n, index)
        copy.start()
        rs_sent.append(copy)

    def rs_take(half, n, index):
        rs_copy(half, n, index).wait_recv()
        return rs_recv[half, n, index].astype(F32)

    def begin(n):
        def body(i, carry):
            half = i % 2
            d = i // 2
            d1 = (d == 0) * 2 + (d == 1) * 1 - (d == 2) * 1
            o = block(half, d1, OFFSETS[n])
            rows = pl.ds(pl.multiple_of(o * SHARD + half * HALF, HALF), HALF)
            part[n % 2, half, d] = jnp.dot(tok_t[rows, :], delta[...], preferred_element_type=F32)
            return carry

        lax.fori_loop(0, 8, body, 0)
        for half in (0, 1):
            rs_start(half, n, 0, part[n % 2, half, 0, :QUARTER])
            rs_start(half, n, 1, part[n % 2, half, 0, QUARTER:])
            rs_start(half, n, 2, part[n % 2, half, 1, QUARTER:])
            rs_start(half, n, 3, part[n % 2, half, 2, :QUARTER])

    def combine(n):
        for half in (0, 1):
            rs_start(half, n, 4, part[n % 2, half, 1, :QUARTER] + rs_take(half, n, 0))
            rs_start(half, n, 5, part[n % 2, half, 2, QUARTER:] + rs_take(half, n, 1))

    def finish(n):
        for half in (0, 1):
            top = part[n % 2, half, 3, :QUARTER] + rs_take(half, n, 3) + rs_take(half, n, 4)
            bottom = part[n % 2, half, 3, QUARTER:] + rs_take(half, n, 2) + rs_take(half, n, 5)
            if n == 0:
                rs_start(half, 4, 0, top)
                rs_start(half, 4, 1, bottom)
            if n == 1:
                rs_start(half, 4, 2, bottom)
                rs_start(half, 4, 4, top + rs_take(half, 4, 0))
            if n == 2:
                rs_start(half, 4, 3, top)
                rs_start(half, 4, 5, bottom + rs_take(half, 4, 1))
            if n == 3:
                top = top + rs_take(half, 4, 3) + rs_take(half, 4, 4)
                bottom = bottom + rs_take(half, 4, 2) + rs_take(half, 4, 5)
                z_send[half * HALF : half * HALF + QUARTER] = top.astype(BF16)
                z_send[half * HALF + QUARTER : (half + 1) * HALF] = bottom.astype(BF16)

    begin(0)
    for n in range(4):
        if n < 3:
            begin(n + 1)
        combine(n)
        finish(n)

    width = SHARD // nz

    def z_rows(i):
        return pl.ds(pl.multiple_of(((z + i) % nz) * width, width), width)

    def z_copy(i):
        return remote(z_send.at[z_rows(i)], z_recv.at[i], zs_sem.at[i], zr_sem.at[i], z_peer(i))

    def z_start(i, carry):
        z_copy(i).start()
        return carry

    def z_add(i, carry):
        z_copy(i).wait_recv()
        return carry + z_recv[i].astype(F32)

    lax.fori_loop(1, nz, z_start, 0)
    total = z_send[z_rows(0), :].astype(F32)
    total = lax.fori_loop(1, nz, z_add, total)
    total = total * (1.0 / math.sqrt(nz * 2 * RING * RING * TOK))

    per = width // 2
    top, bottom = total[:per], total[per:]
    swap_send[...] = jnp.where(core == 0, bottom, top)
    swap = remote(swap_send, swap_recv, core_send.at[5], core_recv.at[5], partner)
    swap.start()
    kept = jnp.where(core == 0, top, bottom)
    swap.wait_recv()
    came = swap_recv[...]
    out[:, :HALF] = jnp.where(core == 0, kept, came)
    out[:, HALF:] = jnp.where(core == 0, came, kept)

    for copy in core_copies:
        copy.wait_send()
    for copy in ag_sent:
        copy.wait_send()
    for copy in rs_sent:
        copy.wait_send()

    def z_sent(i, carry):
        z_copy(i).wait_send()
        return carry

    lax.fori_loop(1, nz, z_sent, 0)
    swap.wait_send()


def local(nz, counts, tokens, queries, values, out_grad, key_codes, key_scales):
    width = SHARD // nz
    return pl.pallas_call(
        functools.partial(kernel, nz),
        out_shape=jax.ShapeDtypeStruct((width // 2, 2 * HALF), F32),
        in_specs=[pl.BlockSpec(memory_space=pltpu.SMEM)]
        + [pl.BlockSpec(memory_space=pl.ANY)] * 6,
        out_specs=pl.BlockSpec(memory_space=pltpu.VMEM),
        scratch_shapes=[
            pltpu.VMEM((SHARD, HALF), BF16),
            pltpu.VMEM((SHARD, 2), F32),
            pltpu.VMEM((2, 8, 128), jnp.int32),
            pltpu.VMEM((2 * TOK, 16 * SHARD), BF16),
            pltpu.VMEM((16 * SHARD, 2 * TOK), BF16),
            pltpu.VMEM((2 * TOK, QW), BF16),
            pltpu.VMEM((2 * TOK, HALF), BF16),
            pltpu.VMEM((2 * TOK, QW), BF16),
            pltpu.VMEM((16, 2, HALF, HALF), BF16),
            pltpu.VMEM((2 * TOK, HALF), F32),
            pltpu.VMEM((2 * TOK, HALF), BF16),
            pltpu.VMEM((2 * TOK, HALF), BF16),
            pltpu.VMEM((2, 2, 4, HALF, HALF), F32),
            pltpu.VMEM((2, 5, 6, QUARTER, HALF), BF16),
            pltpu.VMEM((2, 5, 6, QUARTER, HALF), BF16),
            pltpu.VMEM((SHARD, HALF), BF16),
            pltpu.VMEM((nz, width, HALF), BF16),
            pltpu.VMEM((width // 2, HALF), F32),
            pltpu.VMEM((width // 2, HALF), F32),
            pltpu.SemaphoreType.DMA((6,)),
            pltpu.SemaphoreType.DMA((6,)),
            pltpu.SemaphoreType.DMA((6,)),
            pltpu.SemaphoreType.DMA((40,)),
            pltpu.SemaphoreType.DMA((40,)),
            pltpu.SemaphoreType.DMA((60,)),
            pltpu.SemaphoreType.DMA((60,)),
            pltpu.SemaphoreType.DMA((nz,)),
            pltpu.SemaphoreType.DMA((nz,)),
        ],
        compiler_params=pltpu.CompilerParams(
            collective_id=0,
            has_side_effects=True,
            vmem_limit_bytes=44 * 1024 * 1024,
        ),
        cost_estimate=pl.CostEstimate(
            flops=2_300_000_000, bytes_accessed=6_000_000, transcendentals=140_000
        ),
    )(counts, tokens, queries, values, out_grad, key_codes, key_scales)


def solution(mesh):
    return jax.shard_map(
        functools.partial(local, mesh.shape["dp"] // 2),
        mesh=mesh,
        in_specs=(
            P(("dp", "fsdp")),
            P(("dp", "fsdp"), None),
            P(("dp", "fsdp"), None),
            P(("dp", "fsdp"), None),
            P(("dp", "fsdp"), None),
            P("fsdp", None),
            P("fsdp", None),
        ),
        out_specs=P(("fsdp", "dp"), None),
        check_vma=False,
    )
```

time: 243 us -> 101 us (0.42)
  blocking collectives: 101 us -> 0 us
  Pallas kernels: 0 us -> 92.3 us
  waiting for transfers between devices: 77.9 us -> 0 us
  local copies, waits for them, and re-layouts: 29.2 us -> 7.43 us
  matrix products: 19.7 us -> 0 us
  between operations: 14.2 us -> 0.68 us
    pallas_call x0 -> x1, Pallas kernels: none -> 92.3 us  [local(): pl.pallas_call(functools.partial(kernel, nz), out_shape=jax.ShapeDtypeStr...]
    all_to_all x2 -> x0, blocking collectives: 81.3 us -> none  [the longest x1 47.2 us: local(): lax.all_to_all(section_split.astype(jnp.bfloat16), 'dp', split_axis=0, co...]
    all_gather x2 -> x0, waiting for transfers between devices: 77.2 us -> none  [the longest x1 50.6 us: local(): lax.all_gather(key_codes, 'fsdp', axis=0, tiled=True)]
    dot_general x5 -> x0, matrix products: 19.7 us -> none  [the longest x1 11.4 us: local(): summed = jnp.dot(tokens, weight, preferred_element_type=jnp.float32)]
    all_gather x1 -> x0, blocking collectives: 19.2 us -> none  [local(): lax.all_gather(key_scales.astype(jnp.bfloat16), 'fsdp', axis=0, tiled=True)]
    mul x1 -> x0, local copies, waits for them, and re-layouts: 11 us -> none  [dequantize(): code_rows.astype(jnp.float32).reshape(row_count, blocks, -1)]
    unnamed x17 -> x12, local copies, waits for them, and re-layouts: 13.1 us -> 7.43 us
    all_to_all x1 -> x0, local copies, waits for them, and re-layouts: 2.6 us -> none  [local(): lax.all_to_all(tokens, 'fsdp', split_axis=1, concat_axis=0, tiled=True)]
  transfers between devices with their start and end apart: 2 -> 0, of which waited for: 2 -> 0; matrix products, arithmetic and copies ran while one was open for 12% -> 0% of each run, Pallas kernels for 0% -> 0%
where the time goes in v1:
time: 101 us; the launch traced here: 100 us
  Pallas kernels  92.3 us (91%)
  local copies, waits for them, and re-layouts  7.43 us (7%)
    pallas_call x1, Pallas kernels, local(): pl.pallas_call(functools.partial(kernel, nz), out_shape=jax.ShapeDtypeStr...  92.3 us
    unnamed x12, local copies, waits for them, and re-layouts  7.43 us

profile of v1, /device:TPU:1, one launch (start us, length us, event | category | flops | bytes accessed | tf_op | source)
XLA Modules:
  0.0 100.4 jit_solution(15860538104769959549)
XLA Ops:
  0.7 0.8 copy.8.scales
  1.5 0.0 copy-start
  1.5 1.6 %copy-done = bf16[128,8192]{1,0:T(8,128)(2,1)S(1)} copy-done((bf16[128,8192]{1,0:T(8,128)(2,1)S(1)}, bf16[128,8192]{1,0:T(8,128)(2,1)}, u32[]{:S(2)}) %copy-start) | copy-done | bytes 2097176
  3.1 0.0 copy-start.1
  3.1 1.2 %copy-done.1 = bf16[128,4096]{1,0:T(8,128)(2,1)S(1)} copy-done((bf16[128,4096]{1,0:T(8,128)(2,1)S(1)}, bf16[128,4096]{1,0:T(8,128)(2,1)}, u32[]{:S(2)}) %copy-start.1) | copy-done | bytes 1048600
  4.3 0.0 copy-start.2
  4.3 1.2 %copy-done.2 = bf16[128,4096]{1,0:T(8,128)(2,1)S(1)} copy-done((bf16[128,4096]{1,0:T(8,128)(2,1)S(1)}, bf16[128,4096]{1,0:T(8,128)(2,1)}, u32[]{:S(2)}) %copy-start.2) | copy-done | bytes 1048600
  5.5 0.0 copy-start.3
  5.5 1.0 %copy-done.3 = bf16[512,512]{1,0:T(8,128)(2,1)S(1)} copy-done((bf16[512,512]{1,0:T(8,128)(2,1)S(1)}, bf16[512,512]{1,0:T(8,128)(2,1)}, u32[]{:S(2)}) %copy-start.3) | copy-done | bytes 524312
  6.6 0.0 copy-start.4
  6.6 0.9 copy-done.4
  7.5 92.3 %shard_map.73 = f32[16,512]{1,0:T(8,128)S(1)} custom-call(s32[1]{0:T(128)S(6)} %copy.10.counts, bf16[128,8192]{1,0:T(8,128)(2,1)S(1)} %copy-done, bf16[128,4096]{1,0:T(8,128)(2,1)S(1)} %copy-done.1, bf16[128,512]{1,0:T(8,128)(2,1)S(1)} %copy-done.4, bf16[128,4096]{1,0:T(8,128)(2,1)S(1)} %copy-done.2, bf16[512,512]{1,0:T(8,128)(2,1)S(1)} %copy-done.3, ...), custom_call_target="tpu_custom_call" | custom-call | flops 2300000000 | bytes 6000000 | tf_op jit(solution)/shard_map/pallas_call | solution.py:421
  99.8 0.6 copy.11
Async XLA Ops:
  1.5 1.6 %copy-start = (bf16[128,8192]{1,0:T(8,128)(2,1)S(1)}, bf16[128,8192]{1,0:T(8,128)(2,1)}, u32[]{:S(2)}) copy-start(bf16[128,8192]{1,0:T(8,128)(2,1)} %tokens.1) | copy-start | bytes 6291460
  3.1 1.2 %copy-start.1 = (bf16[128,4096]{1,0:T(8,128)(2,1)S(1)}, bf16[128,4096]{1,0:T(8,128)(2,1)}, u32[]{:S(2)}) copy-start(bf16[128,4096]{1,0:T(8,128)(2,1)} %queries.1) | copy-start | bytes 3145732
  4.3 1.2 %copy-start.2 = (bf16[128,4096]{1,0:T(8,128)(2,1)S(1)}, bf16[128,4096]{1,0:T(8,128)(2,1)}, u32[]{:S(2)}) copy-start(bf16[128,4096]{1,0:T(8,128)(2,1)} %out_grad.1) | copy-start | bytes 3145732
  5.5 1.0 %copy-start.3 = (bf16[512,512]{1,0:T(8,128)(2,1)S(1)}, bf16[512,512]{1,0:T(8,128)(2,1)}, u32[]{:S(2)}) copy-start(bf16[512,512]{1,0:T(8,128)(2,1)} %codes.1) | copy-start | bytes 1572868
  6.6 0.9 copy-start.4

commit v2 on v1

--- a/solution.py
+++ b/solution.py
@@ -20,7 +20,8 @@
 QUARTER = 128
 GROUP = 8
 QW = 2048
-OFFSETS = (2, 1, -1, 0)
+CHUNKS = 4
+WIDE = 4096
 
 
 def kernel(
@@ -44,7 +45,9 @@
     wbuf,
     acc,
     keys,
-    delta,
+    d_send,
+    d_pair,
+    tok_z,
     part,
     rs_send,
     rs_recv,
@@ -61,6 +64,12 @@
     r_recv,
     zs_sem,
     zr_sem,
+    t_send,
+    t_recv,
+    f_send,
+    f_recv,
+    d_ssem,
+    d_rsem,
 ):
     dp = lax.axis_index("dp")
     f = lax.axis_index("fsdp")
@@ -87,6 +96,9 @@
 
     def z_peer(i):
         return (((z + i) % nz) * 2 + core, f)
+
+    parity = z % 2
+    pair = (z_peer(nz + 1 - 2 * parity), z_peer(nz - 1 + 2 * parity))
 
     mine = pl.ds(pl.multiple_of(core * HALF, HALF), HALF)
     theirs = pl.ds(pl.multiple_of(other * HALF, HALF), HALF)
@@ -183,6 +195,44 @@
     for copy in core_copies:
         copy.start()
 
+    def swap_copy(k, q):
+        i = k * CHUNKS + q
+        columns = pl.ds(k * WIDE + q * (WIDE // CHUNKS), WIDE // CHUNKS)
+        into = pl.ds(q * (WIDE // CHUNKS), WIDE // CHUNKS)
+        return remote(
+            tokens.at[:, columns], tok_z.at[k, low, into], t_send.at[i], t_recv.at[i], pair[k]
+        )
+
+    def pass_copy(k, q):
+        i = k * CHUNKS + q
+        into = pl.ds(q * (WIDE // CHUNKS), WIDE // CHUNKS)
+        return remote(
+            tok_z.at[k, low, into], tok_z.at[k, high, into], f_send.at[i], f_recv.at[i], partner
+        )
+
+    for q in range(CHUNKS):
+        for k in (0, 1):
+            swap_copy(k, q).start()
+
+    def pass_on(q):
+        for k in (0, 1):
+            swap_copy(k, q).wait_recv()
+            pass_copy(k, q).start()
+
+    def transpose_pair(q):
+        for k in (0, 1):
+            pass_copy(k, q).wait_recv()
+
+        def body(i, carry):
+            k = i // 4
+            at = q * (WIDE // CHUNKS) + (i % 4) * HALF
+            columns = pl.ds(pl.multiple_of(at, HALF), HALF)
+            rows = pl.ds(pl.multiple_of(k * WIDE + at, HALF), HALF)
+            tok_t[rows, 2 * TOK :] = tok_z[k, :, columns].T
+            return carry
+
+        lax.fori_loop(0, 8, body, 0)
+
     def project(d1, d2):
         def body(half, carry):
             o = block(half, d1, d2)
@@ -195,7 +245,7 @@
     def transpose(first, last):
         def body(k, carry):
             piece = pl.ds(pl.multiple_of(k * HALF, HALF), HALF)
-            tok_t[piece, :] = tok[:, piece].T
+            tok_t[piece, : 2 * TOK] = tok[:, piece].T
             return carry
 
         lax.fori_loop(first, last, body, 0)
@@ -233,6 +283,7 @@
     second_pass(0)
     project(0, -1)
     project(0, 1)
+    pass_on(0)
     for half in (0, 1):
         ag_wait(half, 2, upper)
         ag_wait(half, 3, lower)
@@ -245,13 +296,17 @@
     second_end(0)
     project(0, 2)
     transpose(16, 24)
+    pass_on(1)
     second_pass(2)
     project(1, -1)
     project(1, 1)
     second_end(1)
     project(-1, 2)
     transpose(24, 32)
+    transpose_pair(0)
+    pass_on(2)
     second_pass(3)
+    transpose_pair(1)
     second_end(2)
     project(1, 2)
     project(2, -1)
@@ -270,39 +325,59 @@
     seen = key_at <= query_at
     contract_last = (((1,), (1,)), ((), ()))
 
-    def microbatch(m, carry):
-        rows = pl.ds(pl.multiple_of(m * MB, MB), MB)
-        live = (m % 4) < cnt[m // 4][0:1]
-        for head in range(2):
-            columns = pl.ds(head * HD, HD)
-            start = head * GROUP * HD
-            query = jnp.concatenate(
-                [q2[rows, pl.ds(start + g * HD, HD)] for g in range(GROUP)], axis=0
+    def attend(head, result):
+        columns = pl.ds(pl.multiple_of(head * HD, HD), HD)
+
+        def group(ref, rows):
+            return jnp.concatenate(
+                [
+                    ref[rows, pl.ds(pl.multiple_of((head * GROUP + g) * HD, HD), HD)]
+                    for g in range(GROUP)
+                ],
+                axis=0,
             )
-            grad = jnp.concatenate(
-                [og2[rows, pl.ds(start + g * HD, HD)] for g in range(GROUP)], axis=0
-            )
+
+        def microbatch(m):
+            rows = pl.ds(pl.multiple_of(m * MB, MB), MB)
+            live = (m % 4) < cnt[m // 4][0:1]
+            query = group(q2, rows)
             scores = lax.dot_general(
                 keys[rows, columns], query, contract_last, preferred_element_type=F32
             )
             weights = jnp.where(seen, jnp.exp(scores * inverse), 0.0)
             probs = weights / jnp.sum(weights, axis=0, keepdims=True)
             prob_grad = lax.dot_general(
-                v2[rows, columns], grad, contract_last, preferred_element_type=F32
+                v2[rows, columns], group(og2, rows), contract_last, preferred_element_type=F32
             )
             row_delta = jnp.sum(probs * prob_grad, axis=0, keepdims=True)
             dscore = (probs * (prob_grad - row_delta)).astype(BF16)
             key_grad = jnp.dot(dscore, query, preferred_element_type=F32) * inverse
-            delta[rows, columns] = jnp.where(live, key_grad, 0.0).astype(BF16)
-        return carry
-
-    lax.fori_loop(0, 2 * TOK // MB, microbatch, 0)
-
-    rs_sent = []
+            result[rows, :] = jnp.where(live, key_grad, 0.0).astype(BF16)
+
+        def body(i, carry):
+            microbatch(2 * i)
+            microbatch(2 * i + 1)
+            return carry
+
+        lax.fori_loop(0, TOK // MB, body, 0)
+
+    def delta_copy(k):
+        return remote(d_send, d_pair.at[k, pl.ds(2 * TOK, 2 * TOK)], d_ssem.at[k], d_rsem.at[k], pair[k])
+
+    pass_on(3)
+    attend(1 - parity, d_send)
+    for k in (0, 1):
+        delta_copy(k).start()
+    transpose_pair(2)
+    attend(parity, d_pair.at[0, pl.ds(0, 2 * TOK)])
+    d_pair[1, : 2 * TOK] = d_pair[0, : 2 * TOK]
+    transpose_pair(3)
+    for k in (0, 1):
+        delta_copy(k).wait_recv()
 
     def rs_copy(half, n, index):
         k = (half * 5 + n) * 6 + index
-        axis = 0 if n < 4 else 1
+        axis = 1 if isinstance(n, int) and n == 4 else 0
         return remote(
             rs_send.at[half, n, index],
             rs_recv.at[half, n, index],
@@ -313,40 +388,45 @@
 
     def rs_start(half, n, index, value):
         rs_send[half, n, index] = value.astype(BF16)
-        copy = rs_copy(half, n, index)
-        copy.start()
-        rs_sent.append(copy)
+        rs_copy(half, n, index).start()
 
     def rs_take(half, n, index):
         rs_copy(half, n, index).wait_recv()
         return rs_recv[half, n, index].astype(F32)
 
-    def begin(n):
-        def body(i, carry):
-            half = i % 2
-            d = i // 2
-            d1 = (d == 0) * 2 + (d == 1) * 1 - (d == 2) * 1
-            o = block(half, d1, OFFSETS[n])
-            rows = pl.ds(pl.multiple_of(o * SHARD + half * HALF, HALF), HALF)
-            part[n % 2, half, d] = jnp.dot(tok_t[rows, :], delta[...], preferred_element_type=F32)
-            return carry
-
-        lax.fori_loop(0, 8, body, 0)
-        for half in (0, 1):
-            rs_start(half, n, 0, part[n % 2, half, 0, :QUARTER])
-            rs_start(half, n, 1, part[n % 2, half, 0, QUARTER:])
-            rs_start(half, n, 2, part[n % 2, half, 1, QUARTER:])
-            rs_start(half, n, 3, part[n % 2, half, 2, :QUARTER])
+    def partial(half, d1, d2):
+        o = block(half, d1, d2)
+        rows = pl.ds(pl.multiple_of(o * SHARD + half * HALF, HALF), HALF)
+        return jnp.dot(tok_t[rows, :], d_pair[o // 8], preferred_element_type=F32)
+
+    def begin(n, carry):
+        d2 = jnp.where(n == 3, 0, jnp.where(n == 2, -1, 2 - n))
+        for half in (0, 1):
+            opposite = partial(half, 2, d2)
+            rs_start(half, n, 0, opposite[:QUARTER])
+            rs_start(half, n, 1, opposite[QUARTER:])
+        for half in (0, 1):
+            up = partial(half, 1, d2)
+            rs_start(half, n, 2, up[QUARTER:])
+            part[n, half, 0] = up[:QUARTER]
+            down = partial(half, -1, d2)
+            rs_start(half, n, 3, down[:QUARTER])
+            part[n, half, 1] = down[QUARTER:]
+        for half in (0, 1):
+            own = partial(half, 0, d2)
+            part[n, half, 2] = own[:QUARTER]
+            part[n, half, 3] = own[QUARTER:]
+        return carry
 
     def combine(n):
         for half in (0, 1):
-            rs_start(half, n, 4, part[n % 2, half, 1, :QUARTER] + rs_take(half, n, 0))
-            rs_start(half, n, 5, part[n % 2, half, 2, QUARTER:] + rs_take(half, n, 1))
+            rs_start(half, n, 4, part[n, half, 0] + rs_take(half, n, 0))
+            rs_start(half, n, 5, part[n, half, 1] + rs_take(half, n, 1))
 
     def finish(n):
         for half in (0, 1):
-            top = part[n % 2, half, 3, :QUARTER] + rs_take(half, n, 3) + rs_take(half, n, 4)
-            bottom = part[n % 2, half, 3, QUARTER:] + rs_take(half, n, 2) + rs_take(half, n, 5)
+            top = part[n, half, 2] + rs_take(half, n, 3) + rs_take(half, n, 4)
+            bottom = part[n, half, 3] + rs_take(half, n, 2) + rs_take(half, n, 5)
             if n == 0:
                 rs_start(half, 4, 0, top)
                 rs_start(half, 4, 1, bottom)
@@ -362,12 +442,15 @@
                 z_send[half * HALF : half * HALF + QUARTER] = top.astype(BF16)
                 z_send[half * HALF + QUARTER : (half + 1) * HALF] = bottom.astype(BF16)
 
-    begin(0)
-    for n in range(4):
-        if n < 3:
-            begin(n + 1)
-        combine(n)
-        finish(n)
+    lax.fori_loop(0, 4, begin, 0)
+    combine(0)
+    combine(1)
+    finish(0)
+    combine(2)
+    finish(1)
+    combine(3)
+    finish(2)
+    finish(3)
 
     width = SHARD // nz
 
@@ -381,13 +464,21 @@
         z_copy(i).start()
         return carry
 
+    def z_take(i):
+        z_copy(i).wait_recv()
+        return z_recv[i].astype(F32)
+
     def z_add(i, carry):
-        z_copy(i).wait_recv()
-        return carry + z_recv[i].astype(F32)
+        odd, even = carry
+        return odd + z_take(2 * i - 1), even + z_take(2 * i)
 
     lax.fori_loop(1, nz, z_start, 0)
-    total = z_send[z_rows(0), :].astype(F32)
-    total = lax.fori_loop(1, nz, z_add, total)
+    same = z_send[z_rows(0), :].astype(F32)
+    unlike, same = lax.fori_loop(1, nz // 2, z_add, (jnp.zeros_like(same), same))
+    unlike = unlike + z_take(nz - 1)
+    total = jnp.concatenate(
+        [jnp.where(parity == 0, same, unlike), jnp.where(parity == 0, unlike, same)], axis=1
+    )
     total = total * (1.0 / math.sqrt(nz * 2 * RING * RING * TOK))
 
     per = width // 2
@@ -405,8 +496,19 @@
         copy.wait_send()
     for copy in ag_sent:
         copy.wait_send()
-    for copy in rs_sent:
-        copy.wait_send()
+    for k in (0, 1):
+        delta_copy(k).wait_send()
+        for q in range(CHUNKS):
+            swap_copy(k, q).wait_send()
+            pass_copy(k, q).wait_send()
+
+    def rs_done(n, carry):
+        for half in (0, 1):
+            for index in range(6):
+                rs_copy(half, n, index).wait_send()
+        return carry
+
+    lax.fori_loop(0, 5, rs_done, 0)
 
     def z_sent(i, carry):
         z_copy(i).wait_send()
@@ -422,26 +524,28 @@
         functools.partial(kernel, nz),
         out_shape=jax.ShapeDtypeStruct((width // 2, 2 * HALF), F32),
         in_specs=[pl.BlockSpec(memory_space=pltpu.SMEM)]
-        + [pl.BlockSpec(memory_space=pl.ANY)] * 6,
+        + [pl.BlockSpec(memory_space=pltpu.HBM)] * 6,
         out_specs=pl.BlockSpec(memory_space=pltpu.VMEM),
         scratch_shapes=[
             pltpu.VMEM((SHARD, HALF), BF16),
             pltpu.VMEM((SHARD, 2), F32),
             pltpu.VMEM((2, 8, 128), jnp.int32),
             pltpu.VMEM((2 * TOK, 16 * SHARD), BF16),
-            pltpu.VMEM((16 * SHARD, 2 * TOK), BF16),
+            pltpu.VMEM((16 * SHARD, 4 * TOK), BF16),
             pltpu.VMEM((2 * TOK, QW), BF16),
             pltpu.VMEM((2 * TOK, HALF), BF16),
             pltpu.VMEM((2 * TOK, QW), BF16),
             pltpu.VMEM((16, 2, HALF, HALF), BF16),
             pltpu.VMEM((2 * TOK, HALF), F32),
             pltpu.VMEM((2 * TOK, HALF), BF16),
-            pltpu.VMEM((2 * TOK, HALF), BF16),
-            pltpu.VMEM((2, 2, 4, HALF, HALF), F32),
-            pltpu.VMEM((2, 5, 6, QUARTER, HALF), BF16),
-            pltpu.VMEM((2, 5, 6, QUARTER, HALF), BF16),
-            pltpu.VMEM((SHARD, HALF), BF16),
-            pltpu.VMEM((nz, width, HALF), BF16),
+            pltpu.VMEM((2 * TOK, HD), BF16),
+            pltpu.VMEM((2, 4 * TOK, HD), BF16),
+            pltpu.VMEM((2, 2 * TOK, WIDE), BF16),
+            pltpu.VMEM((4, 2, 4, QUARTER, HD), F32),
+            pltpu.VMEM((2, 5, 6, QUARTER, HD), BF16),
+            pltpu.VMEM((2, 5, 6, QUARTER, HD), BF16),
+            pltpu.VMEM((SHARD, HD), BF16),
+            pltpu.VMEM((nz, width, HD), BF16),
             pltpu.VMEM((width // 2, HALF), F32),
             pltpu.VMEM((width // 2, HALF), F32),
             pltpu.SemaphoreType.DMA((6,)),
@@ -453,11 +557,17 @@
             pltpu.SemaphoreType.DMA((60,)),
             pltpu.SemaphoreType.DMA((nz,)),
             pltpu.SemaphoreType.DMA((nz,)),
+            pltpu.SemaphoreType.DMA((2 * CHUNKS,)),
+            pltpu.SemaphoreType.DMA((2 * CHUNKS,)),
+            pltpu.SemaphoreType.DMA((2 * CHUNKS,)),
+            pltpu.SemaphoreType.DMA((2 * CHUNKS,)),
+            pltpu.SemaphoreType.DMA((2,)),
+            pltpu.SemaphoreType.DMA((2,)),
         ],
         compiler_params=pltpu.CompilerParams(
             collective_id=0,
             has_side_effects=True,
-            vmem_limit_bytes=44 * 1024 * 1024,
+            vmem_limit_bytes=62 * 1024 * 1024,
         ),
         cost_estimate=pl.CostEstimate(
             flops=2_300_000_000, bytes_accessed=6_000_000, transcendentals=140_000

time: 101 us -> 85.1 us (0.84)
  Pallas kernels: 92.3 us -> 81.3 us
  local copies, waits for them, and re-layouts: 7.43 us -> 2.91 us
    pallas_call x1, Pallas kernels: 92.3 us -> 81.3 us  [local(): pl.pallas_call(functools.partial(kernel, nz), out_shape=jax.ShapeDtypeStr...]
    unnamed x12 -> x2, local copies, waits for them, and re-layouts: 7.43 us -> 2.91 us
where the time goes in v2:
time: 85.1 us; the launch traced here: 84.9 us
  Pallas kernels  81.3 us (96%)
  local copies, waits for them, and re-layouts  2.91 us (3%)
    pallas_call x1, Pallas kernels, local(): pl.pallas_call(functools.partial(kernel, nz), out_shape=jax.ShapeDtypeStr...  81.3 us
    unnamed x2, local copies, waits for them, and re-layouts  2.91 us

profile of v2, /device:TPU:1, one launch (start us, length us, event | category | flops | bytes accessed | tf_op | source)
XLA Modules:
  0.0 84.9 jit_solution(10602744264976149043)
XLA Ops:
  0.7 1.5 %copy.8.scales = f32[512,2]{1,0:T(8,128)} copy(f32[512,2]{0,1:T(2,128)} %param.13) | data formatting | bytes 8192 | tf_op args[6]
  2.2 81.3 %shard_map.73 = f32[16,512]{1,0:T(8,128)} custom-call(s32[1]{0:T(128)S(6)} %copy.10.counts, bf16[128,8192]{1,0:T(8,128)(2,1)} %tokens.1, bf16[128,4096]{1,0:T(8,128)(2,1)} %queries.1, bf16[128,512]{1,0:T(8,128)(2,1)} %values.1, bf16[128,4096]{1,0:T(8,128)(2,1)} %out_grad.1, bf16[512,512]{1,0:T(8,128)(2,1)} %codes.1, f32[512,2]{1,0:T(8,128)} %copy.8.scales), custom_call_target="tpu_custom_call" | custom-call | flops 2300000000 | bytes 6000000 | tf_op jit(solution)/shard_map/pallas_call | solution.py:523
  83.5 1.4 %copy.11 = f32[16,512]{1,0:T(8,128)} copy(f32[16,512]{1,0:T(8,128)} %shard_map.73) | data formatting | bytes 65536

commit v3 on v2

--- a/solution.py
+++ b/solution.py
@@ -20,6 +20,7 @@
 QUARTER = 128
 GROUP = 8
 QW = 2048
+OFFSETS = (2, 1, -1, 0)
 CHUNKS = 4
 WIDE = 4096
 
@@ -53,8 +54,6 @@
     rs_recv,
     z_send,
     z_recv,
-    swap_send,
-    swap_recv,
     load_sem,
     core_send,
     core_recv,
@@ -70,6 +69,7 @@
     f_recv,
     d_ssem,
     d_rsem,
+    relay,
 ):
     dp = lax.axis_index("dp")
     f = lax.axis_index("fsdp")
@@ -123,24 +123,22 @@
     cnt[0] = jnp.full((8, 128), counts[0], jnp.int32)
 
     barrier = pltpu.get_barrier_semaphore()
-    neighbours = [partner, chip(1, 0), chip(-1, 0), chip(0, 1), chip(0, -1)]
+    neighbours = [partner, chip(1, 0), chip(-1, 0), chip(0, 1), chip(0, -1), *pair]
     for device in neighbours:
         pl.semaphore_signal(barrier, inc=1, device_id=device, device_id_type=MESH)
 
-    def greet(i, carry):
-        pl.semaphore_signal(barrier, inc=1, device_id=z_peer(i), device_id_type=MESH)
-        return carry
-
-    lax.fori_loop(1, nz, greet, 0)
-
     loads[0].wait()
     loads[1].wait()
-    scale = jnp.where(core == 0, scales_v[:, 0:1], scales_v[:, 1:2])
-    weight = (codes_v[...].astype(F32) * scale).astype(BF16)
-    wbuf[f, 0] = weight[:HALF]
-    wbuf[f, 1] = weight[HALF:]
-
-    pl.semaphore_wait(barrier, len(neighbours) + nz - 1)
+    scale = jnp.where(core == 0, scales_v[0:1], scales_v[1:2])
+    scale = jnp.broadcast_to(scale, (HD, SHARD)).T
+    left = (codes_v[:, :HD].astype(F32) * scale).astype(BF16)
+    right = (codes_v[:, HD:].astype(F32) * scale).astype(BF16)
+    for half in (0, 1):
+        rows = slice(half * HALF, (half + 1) * HALF)
+        wbuf[0, f, half] = jnp.where(parity == 0, right[rows], left[rows])
+        wbuf[1, f, half] = jnp.where(parity == 0, left[rows], right[rows])
+
+    pl.semaphore_wait(barrier, len(neighbours))
 
     def remote(src, dst, send, recv, device):
         return pltpu.make_async_remote_copy(
@@ -156,9 +154,9 @@
     whole = pl.ds(0, HALF)
     ag_sent = []
 
-    def ag_copy(half, index, o, rows, axis, step):
-        k = half * 20 + index
-        ref = wbuf.at[o, half, rows]
+    def ag_copy(p, half, index, o, rows, axis, step):
+        k = (p * 2 + half) * 22 + index
+        ref = wbuf.at[p, o, half, rows]
         return remote(ref, ref, ag_send.at[k], ag_recv.at[k], along(half, axis, step))
 
     def ag_start(*args):
@@ -166,19 +164,37 @@
         copy.start()
         ag_sent.append(copy)
 
-    def ag_wait(half, index, rows):
-        ag_copy(half, index, f, rows, 0, 1).wait_recv()
+    def ag_wait(p, half, index, rows):
+        ag_copy(p, half, index, f, rows, 0, 1).wait_recv()
 
     FIRST = (0, -1, 1, 2)
 
-    def both(half, index, d1, d2, axis):
-        ag_start(half, index, block(half, d1, d2), whole, axis, 1)
-        ag_start(half, index + 1, block(half, d1, d2), whole, axis, -1)
-
-    for half in (0, 1):
-        both(half, 0, 0, 0, 0)
-    for half in (0, 1):
-        both(half, 4, 0, 0, 1)
+    def both(p, half, index, d1, d2, axis):
+        ag_start(p, half, index, block(half, d1, d2), whole, axis, 1)
+        ag_start(p, half, index + 1, block(half, d1, d2), whole, axis, -1)
+
+    def gather_start(p, axis):
+        for half in (0, 1):
+            both(p, half, 4 * axis, 0, 0, axis)
+
+    gather_start(0, 0)
+    gather_start(0, 1)
+    gather_start(1, 0)
+    gather_start(1, 1)
+
+    reach = [1 << r for r in range(nz.bit_length()) if 1 << r < nz // 2]
+
+    def tell(r):
+        pl.semaphore_signal(
+            relay.at[2 * r], inc=1, device_id=z_peer(reach[r]), device_id_type=MESH
+        )
+        pl.semaphore_signal(
+            relay.at[2 * r + 1], inc=1, device_id=z_peer(nz - reach[r]), device_id_type=MESH
+        )
+
+    def hear(r):
+        pl.semaphore_wait(relay.at[2 * r], 1)
+        pl.semaphore_wait(relay.at[2 * r + 1], 1)
 
     core_copies = [
         remote(src, dst, core_send.at[i], core_recv.at[i], partner)
@@ -224,108 +240,80 @@
             pass_copy(k, q).wait_recv()
 
         def body(i, carry):
-            k = i // 4
-            at = q * (WIDE // CHUNKS) + (i % 4) * HALF
-            columns = pl.ds(pl.multiple_of(at, HALF), HALF)
-            rows = pl.ds(pl.multiple_of(k * WIDE + at, HALF), HALF)
+            k = i // 2
+            at = q * (WIDE // CHUNKS) + (i % 2) * SHARD
+            columns = pl.ds(pl.multiple_of(at, SHARD), SHARD)
+            rows = pl.ds(pl.multiple_of(k * WIDE + at, SHARD), SHARD)
             tok_t[rows, 2 * TOK :] = tok_z[k, :, columns].T
             return carry
 
-        lax.fori_loop(0, 8, body, 0)
-
-    def project(d1, d2):
-        def body(half, carry):
-            o = block(half, d1, d2)
-            columns = pl.ds(pl.multiple_of(o * SHARD + half * HALF, HALF), HALF)
-            acc[...] += jnp.dot(tok[:, columns], wbuf[o, half], preferred_element_type=F32)
-            return carry
-
-        lax.fori_loop(0, 2, body, 0)
+        lax.fori_loop(0, 4, body, 0)
+
+    def project(p, *offsets):
+        total = acc[p]
+        for d1, d2 in offsets:
+            for half in (0, 1):
+                o = block(half, d1, d2)
+                columns = pl.ds(pl.multiple_of(o * SHARD + half * HALF, HALF), HALF)
+                total += jnp.dot(tok[:, columns], wbuf[p, o, half], preferred_element_type=F32)
+        acc[p] = total
 
     def transpose(first, last):
         def body(k, carry):
-            piece = pl.ds(pl.multiple_of(k * HALF, HALF), HALF)
+            piece = pl.ds(pl.multiple_of(k * SHARD, SHARD), SHARD)
             tok_t[piece, : 2 * TOK] = tok[:, piece].T
             return carry
 
         lax.fori_loop(first, last, body, 0)
 
-    def first_pass():
-        for half in (0, 1):
-            ag_wait(half, 0, whole)
-            ag_start(half, 2, block(half, -1, 0), upper, 0, 1)
-            both(half, 8, -1, 0, 1)
-            ag_wait(half, 1, whole)
-            ag_start(half, 3, block(half, 1, 0), lower, 0, -1)
-            both(half, 12, 1, 0, 1)
-
-    def second_pass(j):
+    def first_pass(p):
+        for half in (0, 1):
+            ag_wait(p, half, 0, whole)
+            ag_start(p, half, 2, block(half, -1, 0), upper, 0, 1)
+            ag_wait(p, half, 1, whole)
+            ag_start(p, half, 3, block(half, 1, 0), lower, 0, -1)
+
+    def second_start(p):
+        for half in (0, 1):
+            both(p, half, 8, -1, 0, 1)
+            both(p, half, 12, 1, 0, 1)
+
+    def first_end(p):
+        for half in (0, 1):
+            ag_wait(p, half, 2, upper)
+            ag_wait(p, half, 3, lower)
+            o = block(half, 2, 0)
+            ag_start(p, half, 16, o, upper, 1, 1)
+            ag_start(p, half, 17, o, lower, 1, -1)
+            ag_start(p, half, 21, o, lower, 1, 1)
+            ag_start(p, half, 20, o, upper, 1, -1)
+
+    def second_pass(p, j):
         for half in (0, 1):
             base = 4 + 4 * j
-            ag_wait(half, base, whole)
-            ag_start(half, base + 2, block(half, FIRST[j], -1), upper, 1, 1)
-            ag_wait(half, base + 1, whole)
-            ag_start(half, base + 3, block(half, FIRST[j], 1), lower, 1, -1)
-
-    def second_end(j):
-        for half in (0, 1):
-            ag_wait(half, 4 + 4 * j + 2, upper)
-            ag_wait(half, 4 + 4 * j + 3, lower)
-
-    acc[...] = jnp.zeros_like(acc)
-    first_pass()
-    loads[2].wait()
-    core_copies[0].wait_recv()
-    project(0, 0)
-    project(-1, 0)
-    project(1, 0)
-    transpose(0, 8)
-    second_pass(0)
-    project(0, -1)
-    project(0, 1)
-    pass_on(0)
-    for half in (0, 1):
-        ag_wait(half, 2, upper)
-        ag_wait(half, 3, lower)
-        both(half, 16, 2, 0, 1)
-    project(2, 0)
-    transpose(8, 16)
-    second_pass(1)
-    project(-1, -1)
-    project(-1, 1)
-    second_end(0)
-    project(0, 2)
-    transpose(16, 24)
-    pass_on(1)
-    second_pass(2)
-    project(1, -1)
-    project(1, 1)
-    second_end(1)
-    project(-1, 2)
-    transpose(24, 32)
-    transpose_pair(0)
-    pass_on(2)
-    second_pass(3)
-    transpose_pair(1)
-    second_end(2)
-    project(1, 2)
-    project(2, -1)
-    project(2, 1)
-    second_end(3)
-    project(2, 2)
-    keys[...] = acc[...].astype(BF16)
-
-    for load in loads[3:]:
-        load.wait()
-    for copy in core_copies[1:]:
-        copy.wait_recv()
+            ag_wait(p, half, base, whole if j < 3 else upper)
+            ag_start(p, half, base + 2, block(half, FIRST[j], -1), upper, 1, 1)
+            ag_wait(p, half, base + 1, whole if j < 3 else lower)
+            ag_start(p, half, base + 3, block(half, FIRST[j], 1), lower, 1, -1)
+
+    def second_end(p, j):
+        for half in (0, 1):
+            ag_wait(p, half, 4 + 4 * j + 2, upper)
+            ag_wait(p, half, 4 + 4 * j + 3, lower)
+
+    def second_rest(p):
+        for half in (0, 1):
+            ag_wait(p, half, 20, upper)
+            ag_wait(p, half, 21, lower)
+
     inverse = 1.0 / math.sqrt(HD)
     key_at = lax.broadcasted_iota(jnp.int32, (MB, GROUP * MB), 0)
     query_at = lax.broadcasted_iota(jnp.int32, (MB, GROUP * MB), 1) % MB
     seen = key_at <= query_at
     contract_last = (((1,), (1,)), ((), ()))
 
-    def attend(head, result):
+    def attend(p, first, last, result):
+        head = (1 - parity) if p == 0 else parity
         columns = pl.ds(pl.multiple_of(head * HD, HD), HD)
 
         def group(ref, rows):
@@ -342,7 +330,7 @@
             live = (m % 4) < cnt[m // 4][0:1]
             query = group(q2, rows)
             scores = lax.dot_general(
-                keys[rows, columns], query, contract_last, preferred_element_type=F32
+                keys[p, rows, :], query, contract_last, preferred_element_type=F32
             )
             weights = jnp.where(seen, jnp.exp(scores * inverse), 0.0)
             probs = weights / jnp.sum(weights, axis=0, keepdims=True)
@@ -355,21 +343,82 @@
             result[rows, :] = jnp.where(live, key_grad, 0.0).astype(BF16)
 
         def body(i, carry):
-            microbatch(2 * i)
-            microbatch(2 * i + 1)
+            for m in range(4):
+                microbatch(4 * i + m)
             return carry
 
-        lax.fori_loop(0, TOK // MB, body, 0)
+        lax.fori_loop(first, last, body, 0)
 
     def delta_copy(k):
         return remote(d_send, d_pair.at[k, pl.ds(2 * TOK, 2 * TOK)], d_ssem.at[k], d_rsem.at[k], pair[k])
 
-    pass_on(3)
-    attend(1 - parity, d_send)
+    tell(0)
+    acc[...] = jnp.zeros_like(acc)
+    first_pass(0)
+    second_start(0)
+    second_pass(0, 0)
+    hear(0)
+    tell(1)
+    loads[2].wait()
+    core_copies[0].wait_recv()
+    first_pass(1)
+    transpose(0, 2)
+    second_pass(1, 0)
+    transpose(2, 4)
+    first_end(0)
+    second_start(1)
+    project(0, (0, 0), (-1, 0), (1, 0), (0, -1), (0, 1))
+    second_pass(0, 1)
+    transpose(4, 6)
+    second_pass(0, 2)
+    hear(1)
+    tell(2)
+    pass_on(0)
+    transpose(6, 8)
+    first_end(1)
+    project(0, (2, 0), (-1, -1), (-1, 1))
+    second_pass(0, 3)
+    second_end(0, 0)
+    second_end(0, 1)
+    project(0, (1, -1), (1, 1), (0, 2), (-1, 2))
+    transpose(8, 10)
+    pass_on(1)
+    second_pass(1, 1)
+    second_end(0, 2)
+    second_pass(1, 2)
+    second_rest(0)
+    project(0, (1, 2), (2, -1), (2, 1))
+    second_end(0, 3)
+    project(0, (2, 2))
+    keys[0] = acc[0].astype(BF16)
+    for load in loads[3:]:
+        load.wait()
+    for copy in core_copies[1:]:
+        copy.wait_recv()
+    attend(0, 0, 1, d_send)
+    second_pass(1, 3)
+    attend(0, 1, 2, d_send)
     for k in (0, 1):
         delta_copy(k).start()
+    pass_on(2)
+    project(1, (0, 0), (-1, 0), (1, 0), (0, -1), (0, 1), (2, 0))
+    second_end(1, 0)
+    second_end(1, 1)
+    project(1, (-1, -1), (-1, 1), (1, -1), (1, 1), (0, 2), (-1, 2))
+    transpose(10, 16)
+    hear(2)
+    second_end(1, 2)
+    second_rest(1)
+    project(1, (1, 2), (2, -1), (2, 1))
+    transpose_pair(0)
+    transpose_pair(1)
+    second_end(1, 3)
+    project(1, (2, 2))
+    keys[1] = acc[1].astype(BF16)
+    pass_on(3)
+    attend(1, 0, 1, d_pair.at[0, pl.ds(0, 2 * TOK)])
     transpose_pair(2)
-    attend(parity, d_pair.at[0, pl.ds(0, 2 * TOK)])
+    attend(1, 1, 2, d_pair.at[0, pl.ds(0, 2 * TOK)])
     d_pair[1, : 2 * TOK] = d_pair[0, : 2 * TOK]
     transpose_pair(3)
     for k in (0, 1):
@@ -399,8 +448,8 @@
         rows = pl.ds(pl.multiple_of(o * SHARD + half * HALF, HALF), HALF)
         return jnp.dot(tok_t[rows, :], d_pair[o // 8], preferred_element_type=F32)
 
-    def begin(n, carry):
-        d2 = jnp.where(n == 3, 0, jnp.where(n == 2, -1, 2 - n))
+    def begin(n):
+        d2 = OFFSETS[n]
         for half in (0, 1):
             opposite = partial(half, 2, d2)
             rs_start(half, n, 0, opposite[:QUARTER])
@@ -416,7 +465,6 @@
             own = partial(half, 0, d2)
             part[n, half, 2] = own[:QUARTER]
             part[n, half, 3] = own[QUARTER:]
-        return carry
 
     def combine(n):
         for half in (0, 1):
@@ -432,65 +480,73 @@
                 rs_start(half, 4, 1, bottom)
             if n == 1:
                 rs_start(half, 4, 2, bottom)
-                rs_start(half, 4, 4, top + rs_take(half, 4, 0))
+                part[1, half, 2] = top
             if n == 2:
                 rs_start(half, 4, 3, top)
-                rs_start(half, 4, 5, bottom + rs_take(half, 4, 1))
+                part[2, half, 3] = bottom
             if n == 3:
                 top = top + rs_take(half, 4, 3) + rs_take(half, 4, 4)
                 bottom = bottom + rs_take(half, 4, 2) + rs_take(half, 4, 5)
                 z_send[half * HALF : half * HALF + QUARTER] = top.astype(BF16)
                 z_send[half * HALF + QUARTER : (half + 1) * HALF] = bottom.astype(BF16)
 
-    lax.fori_loop(0, 4, begin, 0)
+    begin(0)
+    begin(1)
     combine(0)
+    begin(2)
     combine(1)
+    begin(3)
     finish(0)
     combine(2)
+    combine(3)
     finish(1)
-    combine(3)
     finish(2)
+    for half in (0, 1):
+        rs_start(half, 4, 4, part[1, half, 2] + rs_take(half, 4, 0))
+        rs_start(half, 4, 5, part[2, half, 3] + rs_take(half, 4, 1))
     finish(3)
 
-    width = SHARD // nz
-
-    def z_rows(i):
-        return pl.ds(pl.multiple_of(((z + i) % nz) * width, width), width)
-
-    def z_copy(i):
-        return remote(z_send.at[z_rows(i)], z_recv.at[i], zs_sem.at[i], zr_sem.at[i], z_peer(i))
+    per = SHARD // (2 * nz)
+
+    def z_copy(i, k):
+        to = (z + i) % nz
+        its = core if k == 0 else other
+        rows = pl.ds(pl.multiple_of((2 * to + its) * per, per), per)
+        return remote(
+            z_send.at[rows],
+            z_recv.at[k, i],
+            zs_sem.at[k, i],
+            zr_sem.at[k, i],
+            (2 * to + its, f),
+        )
 
     def z_start(i, carry):
-        z_copy(i).start()
+        away = (i + 1) // 2
+        distance = nz // 2 + jnp.where(i % 2 == 0, away, -away)
+        z_copy(distance, 0).start()
+        z_copy(distance, 1).start()
         return carry
 
-    def z_take(i):
-        z_copy(i).wait_recv()
-        return z_recv[i].astype(F32)
+    def z_take(i, k):
+        z_copy(i, k).wait_recv()
+        return z_recv[k, i].astype(F32)
 
     def z_add(i, carry):
-        odd, even = carry
-        return odd + z_take(2 * i - 1), even + z_take(2 * i)
-
-    lax.fori_loop(1, nz, z_start, 0)
-    same = z_send[z_rows(0), :].astype(F32)
-    unlike, same = lax.fori_loop(1, nz // 2, z_add, (jnp.zeros_like(same), same))
-    unlike = unlike + z_take(nz - 1)
-    total = jnp.concatenate(
-        [jnp.where(parity == 0, same, unlike), jnp.where(parity == 0, unlike, same)], axis=1
-    )
-    total = total * (1.0 / math.sqrt(nz * 2 * RING * RING * TOK))
-
-    per = width // 2
-    top, bottom = total[:per], total[per:]
-    swap_send[...] = jnp.where(core == 0, bottom, top)
-    swap = remote(swap_send, swap_recv, core_send.at[5], core_recv.at[5], partner)
-    swap.start()
-    kept = jnp.where(core == 0, top, bottom)
-    swap.wait_recv()
-    came = swap_recv[...]
-    out[:, :HALF] = jnp.where(core == 0, kept, came)
-    out[:, HALF:] = jnp.where(core == 0, came, kept)
+        return tuple(total + z_take(2 * i + n // 2, n % 2) for n, total in enumerate(carry))
+
+    lax.fori_loop(0, nz - 1, z_start, 0)
+    z_copy(0, 1).start()
+    rows = pl.ds(pl.multiple_of((2 * z + core) * per, per), per)
+    mine_sum = z_send[rows, :].astype(F32)
+    sums = (mine_sum, z_take(0, 1), z_take(1, 0), z_take(1, 1))
+    sums = lax.fori_loop(1, nz // 2, z_add, sums)
+    factor = 1.0 / math.sqrt(nz * 2 * RING * RING * TOK)
+    even = [jnp.where(parity == 0, sums[k], sums[2 + k]) * factor for k in (0, 1)]
+    odd = [jnp.where(parity == 0, sums[2 + k], sums[k]) * factor for k in (0, 1)]
+    out[:, :HD] = jnp.where(core == 0, even[0], even[1])
+    out[:, HD : 2 * HD] = jnp.where(core == 0, odd[0], odd[1])
+    out[:, 2 * HD : 3 * HD] = jnp.where(core == 0, even[1], even[0])
+    out[:, 3 * HD :] = jnp.where(core == 0, odd[1], odd[0])
 
     for copy in core_copies:
         copy.wait_send()
@@ -511,11 +567,12 @@
     lax.fori_loop(0, 5, rs_done, 0)
 
     def z_sent(i, carry):
-        z_copy(i).wait_send()
+        z_copy(i, 0).wait_send()
+        z_copy(i, 1).wait_send()
         return carry
 
+    z_copy(0, 1).wait_send()
     lax.fori_loop(1, nz, z_sent, 0)
-    swap.wait_send()
 
 
 def local(nz, counts, tokens, queries, values, out_grad, key_codes, key_scales):
@@ -528,16 +585,16 @@
         out_specs=pl.BlockSpec(memory_space=pltpu.VMEM),
         scratch_shapes=[
             pltpu.VMEM((SHARD, HALF), BF16),
-            pltpu.VMEM((SHARD, 2), F32),
+            pltpu.VMEM((2, SHARD), F32),
             pltpu.VMEM((2, 8, 128), jnp.int32),
             pltpu.VMEM((2 * TOK, 16 * SHARD), BF16),
             pltpu.VMEM((16 * SHARD, 4 * TOK), BF16),
             pltpu.VMEM((2 * TOK, QW), BF16),
             pltpu.VMEM((2 * TOK, HALF), BF16),
             pltpu.VMEM((2 * TOK, QW), BF16),
-            pltpu.VMEM((16, 2, HALF, HALF), BF16),
-            pltpu.VMEM((2 * TOK, HALF), F32),
-            pltpu.VMEM((2 * TOK, HALF), BF16),
+            pltpu.VMEM((2, 16, 2, HALF, HD), BF16),
+            pltpu.VMEM((2, 2 * TOK, HD), F32),
+            pltpu.VMEM((2, 2 * TOK, HD), BF16),
             pltpu.VMEM((2 * TOK, HD), BF16),
             pltpu.VMEM((2, 4 * TOK, HD), BF16),
             pltpu.VMEM((2, 2 * TOK, WIDE), BF16),
@@ -545,24 +602,23 @@
             pltpu.VMEM((2, 5, 6, QUARTER, HD), BF16),
             pltpu.VMEM((2, 5, 6, QUARTER, HD), BF16),
             pltpu.VMEM((SHARD, HD), BF16),
-            pltpu.VMEM((nz, width, HD), BF16),
-            pltpu.VMEM((width // 2, HALF), F32),
-            pltpu.VMEM((width // 2, HALF), F32),
+            pltpu.VMEM((2, nz, width // 2, HD), BF16),
             pltpu.SemaphoreType.DMA((6,)),
             pltpu.SemaphoreType.DMA((6,)),
             pltpu.SemaphoreType.DMA((6,)),
-            pltpu.SemaphoreType.DMA((40,)),
-            pltpu.SemaphoreType.DMA((40,)),
+            pltpu.SemaphoreType.DMA((88,)),
+            pltpu.SemaphoreType.DMA((88,)),
             pltpu.SemaphoreType.DMA((60,)),
             pltpu.SemaphoreType.DMA((60,)),
-            pltpu.SemaphoreType.DMA((nz,)),
-            pltpu.SemaphoreType.DMA((nz,)),
+            pltpu.SemaphoreType.DMA((2, nz)),
+            pltpu.SemaphoreType.DMA((2, nz)),
             pltpu.SemaphoreType.DMA((2 * CHUNKS,)),
             pltpu.SemaphoreType.DMA((2 * CHUNKS,)),
             pltpu.SemaphoreType.DMA((2 * CHUNKS,)),
             pltpu.SemaphoreType.DMA((2 * CHUNKS,)),
             pltpu.SemaphoreType.DMA((2,)),
             pltpu.SemaphoreType.DMA((2,)),
+            pltpu.SemaphoreType.REGULAR((8,)),
         ],
         compiler_params=pltpu.CompilerParams(
             collective_id=0,
@@ -572,7 +628,7 @@
         cost_estimate=pl.CostEstimate(
             flops=2_300_000_000, bytes_accessed=6_000_000, transcendentals=140_000
         ),
-    )(counts, tokens, queries, values, out_grad, key_codes, key_scales)
+    )(counts, tokens, queries, values, out_grad, key_codes, key_scales.T)
 
 
 def solution(mesh):

time: 85.1 us -> 74.2 us (0.87)
  Pallas kernels: 81.3 us -> 72 us
  local copies, waits for them, and re-layouts: 2.91 us -> 1.38 us
    pallas_call x1, Pallas kernels: 81.3 us -> 72 us  [local(): pl.pallas_call(functools.partial(kernel, nz), out_shape=jax.ShapeDtypeStr...]
    unnamed x2 -> x1, local copies, waits for them, and re-layouts: 2.91 us -> 1.38 us
where the time goes in v3:
time: 74.2 us; the launch traced here: 74 us
  Pallas kernels  72 us (97%)
  local copies, waits for them, and re-layouts  1.38 us (2%)
    pallas_call x1, Pallas kernels, local(): pl.pallas_call(functools.partial(kernel, nz), out_shape=jax.ShapeDtypeStr...  72 us

profile of v3, /device:TPU:1, one launch (start us, length us, event | category | flops | bytes accessed | tf_op | source)
XLA Modules:
  0.0 74.0 jit_solution(5362946708245205639)
XLA Ops:
  0.7 72.0 %shard_map.73 = f32[16,512]{1,0:T(8,128)} custom-call(s32[1]{0:T(128)S(6)} %copy.9.counts, bf16[128,8192]{1,0:T(8,128)(2,1)} %tokens.1, bf16[128,4096]{1,0:T(8,128)(2,1)} %queries.1, bf16[128,512]{1,0:T(8,128)(2,1)} %values.1, bf16[128,4096]{1,0:T(8,128)(2,1)} %out_grad.1, bf16[512,512]{1,0:T(8,128)(2,1)} %codes.1, f32[2,512]{1,0:T(2,128)} %bitcast.1), custom_call_target="tpu_custom_call" | custom-call | flops 2300000000 | bytes 6000000 | tf_op jit(solution)/shard_map/pallas_call | solution.py:580
  72.7 1.4 %copy.10 = f32[16,512]{1,0:T(8,128)} copy(f32[16,512]{1,0:T(8,128)} %shard_map.73) | data formatting | bytes 65536

commit v4 on v3

--- a/solution.py
+++ b/solution.py
@@ -100,6 +100,11 @@
     parity = z % 2
     pair = (z_peer(nz + 1 - 2 * parity), z_peer(nz - 1 + 2 * parity))
 
+    barrier = pltpu.get_barrier_semaphore()
+    neighbours = [partner, chip(1, 0), chip(-1, 0), chip(0, 1), chip(0, -1), *pair]
+    for device in neighbours:
+        pl.semaphore_signal(barrier, inc=1, device_id=device, device_id_type=MESH)
+
     mine = pl.ds(pl.multiple_of(core * HALF, HALF), HALF)
     theirs = pl.ds(pl.multiple_of(other * HALF, HALF), HALF)
     mine_q = pl.ds(pl.multiple_of(core * QW, QW), QW)
@@ -118,15 +123,8 @@
             ]
         )
     ]
-    for load in loads:
+    for load in loads[:2]:
         load.start()
-    cnt[0] = jnp.full((8, 128), counts[0], jnp.int32)
-
-    barrier = pltpu.get_barrier_semaphore()
-    neighbours = [partner, chip(1, 0), chip(-1, 0), chip(0, 1), chip(0, -1), *pair]
-    for device in neighbours:
-        pl.semaphore_signal(barrier, inc=1, device_id=device, device_id_type=MESH)
-
     loads[0].wait()
     loads[1].wait()
     scale = jnp.where(core == 0, scales_v[0:1], scales_v[1:2])
@@ -138,6 +136,8 @@
         wbuf[0, f, half] = jnp.where(parity == 0, right[rows], left[rows])
         wbuf[1, f, half] = jnp.where(parity == 0, left[rows], right[rows])
 
+    for load in loads[2:]:
+        load.start()
     pl.semaphore_wait(barrier, len(neighbours))
 
     def remote(src, dst, send, recv, device):
@@ -179,6 +179,18 @@
 
     gather_start(0, 0)
     gather_start(0, 1)
+    def swap_copy(k, q):
+        i = k * CHUNKS + q
+        columns = pl.ds(k * WIDE + q * (WIDE // CHUNKS), WIDE // CHUNKS)
+        into = pl.ds(q * (WIDE // CHUNKS), WIDE // CHUNKS)
+        return remote(
+            tokens.at[:, columns], tok_z.at[k, low, into], t_send.at[i], t_recv.at[i], pair[k]
+        )
+
+    for q in range(CHUNKS):
+        for k in (0, 1):
+            swap_copy(k, q).start()
+
     gather_start(1, 0)
     gather_start(1, 1)
 
@@ -208,16 +220,8 @@
             ]
         )
     ]
-    for copy in core_copies:
+    for copy in core_copies[:4]:
         copy.start()
-
-    def swap_copy(k, q):
-        i = k * CHUNKS + q
-        columns = pl.ds(k * WIDE + q * (WIDE // CHUNKS), WIDE // CHUNKS)
-        into = pl.ds(q * (WIDE // CHUNKS), WIDE // CHUNKS)
-        return remote(
-            tokens.at[:, columns], tok_z.at[k, low, into], t_send.at[i], t_recv.at[i], pair[k]
-        )
 
     def pass_copy(k, q):
         i = k * CHUNKS + q
@@ -225,10 +229,6 @@
         return remote(
             tok_z.at[k, low, into], tok_z.at[k, high, into], f_send.at[i], f_recv.at[i], partner
         )
-
-    for q in range(CHUNKS):
-        for k in (0, 1):
-            swap_copy(k, q).start()
 
     def pass_on(q):
         for k in (0, 1):
@@ -353,6 +353,8 @@
         return remote(d_send, d_pair.at[k, pl.ds(2 * TOK, 2 * TOK)], d_ssem.at[k], d_rsem.at[k], pair[k])
 
     tell(0)
+    cnt[0] = jnp.full((8, 128), counts[0], jnp.int32)
+    core_copies[4].start()
     acc[...] = jnp.zeros_like(acc)
     first_pass(0)
     second_start(0)
@@ -412,13 +414,12 @@
     project(1, (1, 2), (2, -1), (2, 1))
     transpose_pair(0)
     transpose_pair(1)
+    pass_on(3)
+    transpose_pair(2)
     second_end(1, 3)
     project(1, (2, 2))
     keys[1] = acc[1].astype(BF16)
-    pass_on(3)
-    attend(1, 0, 1, d_pair.at[0, pl.ds(0, 2 * TOK)])
-    transpose_pair(2)
-    attend(1, 1, 2, d_pair.at[0, pl.ds(0, 2 * TOK)])
+    attend(1, 0, 2, d_pair.at[0, pl.ds(0, 2 * TOK)])
     d_pair[1, : 2 * TOK] = d_pair[0, : 2 * TOK]
     transpose_pair(3)
     for k in (0, 1):
@@ -448,21 +449,24 @@
         rows = pl.ds(pl.multiple_of(o * SHARD + half * HALF, HALF), HALF)
         return jnp.dot(tok_t[rows, :], d_pair[o // 8], preferred_element_type=F32)
 
-    def begin(n):
-        d2 = OFFSETS[n]
-        for half in (0, 1):
-            opposite = partial(half, 2, d2)
-            rs_start(half, n, 0, opposite[:QUARTER])
-            rs_start(half, n, 1, opposite[QUARTER:])
-        for half in (0, 1):
-            up = partial(half, 1, d2)
+    def opposite(n):
+        for half in (0, 1):
+            value = partial(half, 2, OFFSETS[n])
+            rs_start(half, n, 0, value[:QUARTER])
+            rs_start(half, n, 1, value[QUARTER:])
+
+    def sides(n):
+        for half in (0, 1):
+            up = partial(half, 1, OFFSETS[n])
             rs_start(half, n, 2, up[QUARTER:])
             part[n, half, 0] = up[:QUARTER]
-            down = partial(half, -1, d2)
+            down = partial(half, -1, OFFSETS[n])
             rs_start(half, n, 3, down[:QUARTER])
             part[n, half, 1] = down[QUARTER:]
-        for half in (0, 1):
-            own = partial(half, 0, d2)
+
+    def stay(n):
+        for half in (0, 1):
+            own = partial(half, 0, OFFSETS[n])
             part[n, half, 2] = own[:QUARTER]
             part[n, half, 3] = own[QUARTER:]
 
@@ -490,15 +494,23 @@
                 z_send[half * HALF : half * HALF + QUARTER] = top.astype(BF16)
                 z_send[half * HALF + QUARTER : (half + 1) * HALF] = bottom.astype(BF16)
 
-    begin(0)
-    begin(1)
+    opposite(0)
+    sides(0)
+    opposite(1)
+    sides(1)
+    opposite(2)
+    stay(0)
     combine(0)
-    begin(2)
+    sides(2)
+    opposite(3)
     combine(1)
-    begin(3)
+    stay(1)
+    stay(2)
+    combine(2)
     finish(0)
-    combine(2)
+    sides(3)
     combine(3)
+    stay(3)
     finish(1)
     finish(2)
     for half in (0, 1):
@@ -536,6 +548,24 @@
 
     lax.fori_loop(0, nz - 1, z_start, 0)
     z_copy(0, 1).start()
+    for copy in core_copies:
+        copy.wait_send()
+    for copy in ag_sent:
+        copy.wait_send()
+    for k in (0, 1):
+        delta_copy(k).wait_send()
+        for q in range(CHUNKS):
+            swap_copy(k, q).wait_send()
+            pass_copy(k, q).wait_send()
+
+    def rs_done(n, carry):
+        for half in (0, 1):
+            for index in range(6):
+                rs_copy(half, n, index).wait_send()
+        return carry
+
+    lax.fori_loop(0, 5, rs_done, 0)
+
     rows = pl.ds(pl.multiple_of((2 * z + core) * per, per), per)
     mine_sum = z_send[rows, :].astype(F32)
     sums = (mine_sum, z_take(0, 1), z_take(1, 0), z_take(1, 1))
@@ -547,24 +577,6 @@
     out[:, HD : 2 * HD] = jnp.where(core == 0, odd[0], odd[1])
     out[:, 2 * HD : 3 * HD] = jnp.where(core == 0, even[1], even[0])
     out[:, 3 * HD :] = jnp.where(core == 0, odd[1], odd[0])
-
-    for copy in core_copies:
-        copy.wait_send()
-    for copy in ag_sent:
-        copy.wait_send()
-    for k in (0, 1):
-        delta_copy(k).wait_send()
-        for q in range(CHUNKS):
-            swap_copy(k, q).wait_send()
-            pass_copy(k, q).wait_send()
-
-    def rs_done(n, carry):
-        for half in (0, 1):
-            for index in range(6):
-                rs_copy(half, n, index).wait_send()
-        return carry
-
-    lax.fori_loop(0, 5, rs_done, 0)
 
     def z_sent(i, carry):
         z_copy(i, 0).wait_send()

time: 74.2 us -> 73 us (0.984)
  Pallas kernels: 72 us -> 70.7 us
    pallas_call x1, Pallas kernels: 72 us -> 70.7 us  [local(): pl.pallas_call(functools.partial(kernel, nz), out_shape=jax.ShapeDtypeStr...]
where the time goes in v4:
time: 73 us; the launch traced here: 72.8 us
  Pallas kernels  70.7 us (97%)
  local copies, waits for them, and re-layouts  1.38 us (2%)
    pallas_call x1, Pallas kernels, local(): pl.pallas_call(functools.partial(kernel, nz), out_shape=jax.ShapeDtypeStr...  70.7 us

profile of v4, /device:TPU:1, one launch (start us, length us, event | category | flops | bytes accessed | tf_op | source)
XLA Modules:
  0.0 72.8 jit_solution(9742224028538594504)
XLA Ops:
  0.7 70.7 %shard_map.73 = f32[16,512]{1,0:T(8,128)} custom-call(s32[1]{0:T(128)S(6)} %copy.9.counts, bf16[128,8192]{1,0:T(8,128)(2,1)} %tokens.1, bf16[128,4096]{1,0:T(8,128)(2,1)} %queries.1, bf16[128,512]{1,0:T(8,128)(2,1)} %values.1, bf16[128,4096]{1,0:T(8,128)(2,1)} %out_grad.1, bf16[512,512]{1,0:T(8,128)(2,1)} %codes.1, f32[2,512]{1,0:T(2,128)} %bitcast.1), custom_call_target="tpu_custom_call" | custom-call | flops 2300000000 | bytes 6000000 | tf_op jit(solution)/shard_map/pallas_call | solution.py:592
  71.4 1.4 %copy.10 = f32[16,512]{1,0:T(8,128)} copy(f32[16,512]{1,0:T(8,128)} %shard_map.73) | data formatting | bytes 65536

commit v5 on v4

--- a/solution.py
+++ b/solution.py
@@ -22,6 +22,7 @@
 QW = 2048
 OFFSETS = (2, 1, -1, 0)
 CHUNKS = 4
+FROM = (0, 1024, 2048, 3584, 4096)
 WIDE = 4096
 
 
@@ -181,8 +182,8 @@
     gather_start(0, 1)
     def swap_copy(k, q):
         i = k * CHUNKS + q
-        columns = pl.ds(k * WIDE + q * (WIDE // CHUNKS), WIDE // CHUNKS)
-        into = pl.ds(q * (WIDE // CHUNKS), WIDE // CHUNKS)
+        columns = pl.ds(k * WIDE + FROM[q], FROM[q + 1] - FROM[q])
+        into = pl.ds(FROM[q], FROM[q + 1] - FROM[q])
         return remote(
             tokens.at[:, columns], tok_z.at[k, low, into], t_send.at[i], t_recv.at[i], pair[k]
         )
@@ -225,7 +226,7 @@
 
     def pass_copy(k, q):
         i = k * CHUNKS + q
-        into = pl.ds(q * (WIDE // CHUNKS), WIDE // CHUNKS)
+        into = pl.ds(FROM[q], FROM[q + 1] - FROM[q])
         return remote(
             tok_z.at[k, low, into], tok_z.at[k, high, into], f_send.at[i], f_recv.at[i], partner
         )
@@ -240,14 +241,15 @@
             pass_copy(k, q).wait_recv()
 
         def body(i, carry):
-            k = i // 2
-            at = q * (WIDE // CHUNKS) + (i % 2) * SHARD
+            k = i // pieces
+            at = FROM[q] + (i % pieces) * SHARD
             columns = pl.ds(pl.multiple_of(at, SHARD), SHARD)
             rows = pl.ds(pl.multiple_of(k * WIDE + at, SHARD), SHARD)
             tok_t[rows, 2 * TOK :] = tok_z[k, :, columns].T
             return carry
 
-        lax.fori_loop(0, 4, body, 0)
+        pieces = (FROM[q + 1] - FROM[q]) // SHARD
+        lax.fori_loop(0, 2 * pieces, body, 0)
 
     def project(p, *offsets):
         total = acc[p]

time: 73 us -> 72.8 us (level)
  no operation moved by 1% of the time
where the time goes in v5:
time: 72.8 us; the launch traced here: 72.6 us
  Pallas kernels  70.5 us (97%)
  local copies, waits for them, and re-layouts  1.38 us (2%)
    pallas_call x1, Pallas kernels, local(): pl.pallas_call(functools.partial(kernel, nz), out_shape=jax.ShapeDtypeStr...  70.5 us

profile of v5, /device:TPU:1, one launch (start us, length us, event | category | flops | bytes accessed | tf_op | source)
XLA Modules:
  0.0 72.6 jit_solution(10761497759515301901)
XLA Ops:
  0.7 70.5 %shard_map.73 = f32[16,512]{1,0:T(8,128)} custom-call(s32[1]{0:T(128)S(6)} %copy.9.counts, bf16[128,8192]{1,0:T(8,128)(2,1)} %tokens.1, bf16[128,4096]{1,0:T(8,128)(2,1)} %queries.1, bf16[128,512]{1,0:T(8,128)(2,1)} %values.1, bf16[128,4096]{1,0:T(8,128)(2,1)} %out_grad.1, bf16[512,512]{1,0:T(8,128)(2,1)} %codes.1, f32[2,512]{1,0:T(2,128)} %bitcast.1), custom_call_target="tpu_custom_call" | custom-call | flops 2300000000 | bytes 6000000 | tf_op jit(solution)/shard_map/pallas_call | solution.py:594
  71.2 1.4 %copy.10 = f32[16,512]{1,0:T(8,128)} copy(f32[16,512]{1,0:T(8,128)} %shard_map.73) | data formatting | bytes 65536
